TPU v7x, 128 devices: a whole 4x4x4 slice. The times are simulated.
128 devices in a mesh: dp: 16 (over x_lo, y, core), tensor: 8 (over x_hi, z).
Axes of the slice: x: 4 (x_hi: 2, x_lo: 2; x = x_hi * 2 + x_lo), y: 4, z: 4, core: 2. Of those that a mesh axis runs over, the one named last changes fastest.
Arguments:
- activations: bfloat16 [4096, 14336], P('dp', 'tensor'), may hold values from -6 to 6
- quant_act: bfloat16 [4096, 14336], P('dp', 'tensor'), may hold values from -6 to 6
- act_scale: float32 [4096, 112], P('dp', 'tensor'), may hold values from 0.1 to 1
- act_mask: int32 [4096, 14336], P('dp', 'tensor'), may hold values 0 or 1
- quant_weight: bfloat16 [4096, 14336], P('dp', 'tensor'), may hold values from -0.046875 to 0.046875
- weight_mask: int32 [4096, 14336], P('dp', 'tensor'), may hold values 0 or 1
- grad_out: bfloat16 [4096, 4096], P('dp'), may hold values from -6 to 6
Outputs:
- grad_act: bfloat16 [4096, 14336], P('dp', 'tensor')
- grad_scale: float32 [4096, 112], P('dp', 'tensor')
- grad_weight: bfloat16 [4096, 14336], P('dp', 'tensor')
All inputs are finite; a program needn't handle non-finite values. No bound on the sum of `act_mask` or of `weight_mask` on one device may be relied on, other than what follows from the above.
Results may differ from a plain program's by a relative error of at most 0.023.
Values may be sent and summed in bfloat16 or wider, within the bound.
A program may use at most 128 MiB of HBM per device.

v0:
```python
import math

import jax
import jax.numpy as jnp
from jax import lax
from jax.sharding import PartitionSpec as P

GROUP = 128


def partner_2(value, axis, apart):
    mask = 2**apart
    pairs = [(source, source ^ mask) for source in range(lax.axis_size(axis))]
    return lax.ppermute(value, axis, pairs)


def sign_signs(count):
    index = jnp.arange(count)
    table = jnp.ones((count, count), jnp.float32)
    for level in range(count.bit_length() - 1):
        bit_row = index // 2**level % 2
        table = table * (1.0 - 2.0 * (bit_row[:, None] * bit_row[None, :]).astype(jnp.float32))
    return table


def local_mix_narrow(values):
    rows, width = values.shape
    blocks = values.reshape(rows, width // GROUP, GROUP)
    signs = sign_signs(GROUP).astype(jnp.bfloat16)
    mixed = jnp.einsum("tbj,jk->tbk", blocks, signs, preferred_element_type=jnp.float32)
    return mixed.reshape(rows, width) * (1.0 / math.sqrt(GROUP))


def local_mix_wide(values):
    rows, width = values.shape
    blocks = values.reshape(rows, width // GROUP, GROUP)
    mixed = jnp.einsum("tbj,jk->tbk", blocks, sign_signs(GROUP), precision=lax.Precision.HIGH)
    return mixed.reshape(rows, width) * (1.0 / math.sqrt(GROUP))


def cross_mix(values):
    count = lax.axis_size("tensor")
    position = lax.axis_index("tensor")
    for level in range(count.bit_length() - 1):
        partner = partner_2(values.astype(jnp.bfloat16), "tensor", level).astype(values.dtype)
        upper = position // 2**level % 2
        values = jnp.where(upper == 1, partner - values, values + partner)
    return values / math.sqrt(count)


def shards(activations, quant_act, act_scale, act_mask, quant_weight, weight_mask, grad_out):
    rows = activations.shape[0]
    width = activations.shape[1]
    rotated = cross_mix(local_mix_narrow(activations))
    columns = grad_out
    grad_quant = jnp.dot(
        columns,
        lax.all_gather(quant_weight, "dp", axis=0, tiled=True),
        preferred_element_type=jnp.float32,
    )
    mask_float = act_mask.astype(jnp.float32)
    grad_act = cross_mix(local_mix_wide(mask_float * grad_quant)).astype(jnp.bfloat16)
    spread = grad_quant * (quant_act.astype(jnp.float32) - mask_float * rotated)
    grouped = jnp.sum(spread.reshape(rows, width // GROUP, GROUP), axis=2)
    grad_scale = grouped / (act_scale * math.sqrt(7.0 * GROUP))
    columns = grad_out
    summed = lax.psum_scatter(
        lax.dot_general(
            columns, quant_act, (((0,), (0,)), ((), ())), preferred_element_type=jnp.float32
        ).astype(jnp.bfloat16),
        "dp",
        scatter_dimension=0,
        tiled=True,
    ).astype(jnp.float32)
    grad_weight = (weight_mask.astype(jnp.float32) * summed).astype(jnp.bfloat16)
    return (grad_act, grad_scale, grad_weight)


def solution(mesh):
    return jax.shard_map(
        shards,
        mesh=mesh,
        in_specs=(
            P("dp", "tensor"),
            P("dp", "tensor"),
            P("dp", "tensor"),
            P("dp", "tensor"),
            P("dp", "tensor"),
            P("dp", "tensor"),
            P("dp", None),
        ),
        out_specs=(P("dp", "tensor"), P("dp", "tensor"), P("dp", "tensor")),
        check_vma=False,
    )
```

profile of v0, /device:TPU:4, one launch (start us, length us, event | category | flops | bytes accessed | tf_op | source)
XLA Modules:
  0.0 228.4 jit_solution(976640499339573390)
XLA Ops:
  7.2 0.7 all-gather.2.cloned.1.call-update
  8.0 0.8 copy-done
  8.8 8.5 %convolution_convert_fusion = bf16[4096,1792]{1,0:T(8,128)(2,1)} fusion(bf16[256,4096]{1,0:T(8,128)(2,1)S(1)} %copy-done, bf16[256,1792]{1,0:T(8,128)(2,1)} %param.8), kind=kOutput, calls=%fused_computation | convolution fusion | flops 3765436416 | bytes 17694720 | tf_op jit(solution)/shard_map/dot_general | solution.py:68
  17.3 1.5 copy.19
  18.8 1.8 convolution_multiply_fusion
  20.6 3.2 %copy.21 = f32[256,1792]{1,0:T(8,128)} copy(f32[256,1792]{0,1:T(8,128)} %bitcast.22) | data formatting | bytes 3670016 | tf_op jit(solution)/shard_map/mul | solution.py:31
  23.8 2.5 %convert_element_type.119 = bf16[256,1792]{1,0:T(8,128)(2,1)} convert(f32[256,1792]{1,0:T(8,128)} %copy.21) | non-fusion elementwise | flops 458752 | bytes 2752512 | tf_op jit(solution)/shard_map/convert_element_type | solution.py:45
  26.3 1.7 collective-permute-start.3
  28.0 20.8 %collective-permute-done.3 = bf16[256,1792]{1,0:T(8,128)(2,1)S(1)} collective-permute-done((bf16[256,1792]{1,0:T(8,128)(2,1)}, bf16[256,1792]{1,0:T(8,128)(2,1)S(1)}, u32[]{:S(2)}, u32[]{:S(2)}) %collective-permute-start.3) | collective-permute-done | bytes 917536 | tf_op jit(solution)/shard_map/ppermute | solution.py:14
  48.8 2.7 %fusion.14 = bf16[256,1792]{1,0:T(8,128)(2,1)} fusion(f32[256,1792]{1,0:T(8,128)} %copy.21, bf16[256,1792]{1,0:T(8,128)(2,1)S(1)} %collective-permute-done.3, pred[]{:T(512)S(6)} %eq.36), kind=kLoop, calls=%fused_computation.31 | loop fusion | flops 2293760 | bytes 3670017 | tf_op jit(solution)/shard_map/convert_element_type | solution.py:45
  51.5 3.4 %collective-permute-start.4 = (bf16[256,1792]{1,0:T(8,128)(2,1)}, bf16[256,1792]{1,0:T(8,128)(2,1)}, u32[]{:S(2)}, u32[]{:S(2)}) collective-permute-start(bf16[256,1792]{1,0:T(8,128)(2,1)} %fusion.14), channel_id=1, source_target_pairs={{0,2},{1,3},{2,0},{3,1},{4,6},{5,7},{6,4},{7,5},{8,10},{9,11},{10,... | collective-permute-start | bytes 2752520 | tf_op jit(solution)/shard_map/ppermute | solution.py:14
  55.0 20.0 %collective-permute-done.4 = bf16[256,1792]{1,0:T(8,128)(2,1)} collective-permute-done((bf16[256,1792]{1,0:T(8,128)(2,1)}, bf16[256,1792]{1,0:T(8,128)(2,1)}, u32[]{:S(2)}, u32[]{:S(2)}) %collective-permute-start.4) | collective-permute-done | bytes 917536 | tf_op jit(solution)/shard_map/ppermute | solution.py:14
  75.0 3.3 %fusion.12 = bf16[256,1792]{1,0:T(8,128)(2,1)} fusion(bf16[256,1792]{1,0:T(8,128)(2,1)} %collective-permute-done.4, pred[]{:T(512)S(6)} %eq.35, f32[256,1792]{1,0:T(8,128)} %copy.21, bf16[256,1792]{1,0:T(8,128)(2,1)S(1)} %collective-permute-done.3, pred[]{:T(512)S(6)} %eq.36), kind=kLoop, calls=%fused_computation.29 | loop fusion | flops 4128768 | bytes 4587522 | tf_op jit(solution)/shard_map/convert_element_type | solution.py:45
  78.3 0.6 collective-permute-start.5
  78.9 25.4 %all-gather.2.cloned.1.call-done = bf16[4096,1792]{1,0:T(8,128)(2,1)} async-done(((bf16[256,1792]{1,0:T(8,128)(2,1)}), bf16[4096,1792]{1,0:T(8,128)(2,1)}) %all-gather.2.cloned.1.call-update) | async-done | bytes 14680080 | tf_op jit(solution)/shard_map/all_gather | solution.py:58
  104.3 7.9 %fusion.29 = f32[256,1792]{1,0:T(8,128)S(1)} fusion(bf16[256,4096]{1,0:T(8,128)(2,1)S(1)} %copy-done, bf16[4096,1792]{1,0:T(8,128)(2,1)} %all-gather.2.cloned.1.call-done), kind=kOutput, calls=%fused_computation.85 | convolution fusion | flops 3758096384 | bytes 18612224 | tf_op jit(solution)/shard_map/dot_general | solution.py:56
  112.3 4.5 %fusion.11 = (f32[256,1792]{1,0:T(8,128)}, f32[256,1792]{1,0:T(8,128)}) fusion(f32[256,1792]{1,0:T(8,128)S(1)} %fusion.29, bf16[256,1792]{1,0:T(8,128)(2,1)} %collective-permute-done.5, bf16[256,1792]{1,0:T(8,128)(2,1)S(1)} %copy-done.7, s32[256,1792]{1,0:T(8,128)S(1)} %copy-done.8, bf16[256,1792]{1,0:T(8,128)(2,1)} %collective-permute-done.4, pred[]{:T(512)S(6)} %eq.35, ...), kind=kLoop, calls=%fused_computation.24 | loop fusion | flops 8716288 | bytes 12845059 | tf_op jit(solution)/shard_map/mul | solution.py:63
  116.7 2.0 copy.14
  118.7 2.3 %convolution_multiply_fusion.1 = f32[256,14,128]{0,2,1:T(8,128)} fusion(f32[256,14,128]{0,2,1:T(8,128)S(1)} %bitcast.19, s32[128]{0:T(128)S(1)} %get-tuple-element.5, s32[128]{0:T(128)S(1)} %get-tuple-element.6, s32[128]{0:T(128)S(1)} %get-tuple-element.7, s32[128]{0:T(128)S(1)} %get-tuple-element.8, s32[128]{0:T(128)S(1)} %get-tuple-element.9, ...), kind=kOutput, calls=%fused_computation.28 | convolution fusion | flops 353337344 | bytes 3673600 | tf_op jit(solution)/shard_map/tbj,jk->tbk/dot_general | solution.py:37
  121.0 1.8 copy.16
  122.9 1.6 collective-permute-start
  124.6 20.9 %collective-permute-done = bf16[256,1792]{1,0:T(8,128)(2,1)S(1)} collective-permute-done((bf16[256,1792]{1,0:T(8,128)(2,1)S(1)}, bf16[256,1792]{1,0:T(8,128)(2,1)S(1)}, u32[]{:S(2)}, u32[]{:S(2)}) %collective-permute-start) | collective-permute-done | bytes 917536 | tf_op jit(solution)/shard_map/ppermute | solution.py:14
  145.5 0.3 fusion.15
  145.8 3.3 %collective-permute-start.1 = (bf16[256,1792]{1,0:T(8,128)(2,1)S(1)}, bf16[256,1792]{1,0:T(8,128)(2,1)S(1)}, u32[]{:S(2)}, u32[]{:S(2)}) collective-permute-start(bf16[256,1792]{1,0:T(8,128)(2,1)S(1)} %fusion.15), channel_id=1, source_target_pairs={{0,2},{1,3},{2,0},{3,1},{4,6},{5,7},{6,4},{7,5},{8,10},{9,11},{10,... | collective-permute-start | bytes 2752520 | tf_op jit(solution)/shard_map/ppermute | solution.py:14
  149.1 20.1 %collective-permute-done.1 = bf16[256,1792]{1,0:T(8,128)(2,1)S(1)} collective-permute-done((bf16[256,1792]{1,0:T(8,128)(2,1)S(1)}, bf16[256,1792]{1,0:T(8,128)(2,1)S(1)}, u32[]{:S(2)}, u32[]{:S(2)}) %collective-permute-start.1) | collective-permute-done | bytes 917536 | tf_op jit(solution)/shard_map/ppermute | solution.py:14
  169.2 1.5 fusion.13
  170.6 1.8 copy.24
  172.6 0.6 copy-done.9
  173.2 0.6 multiply_divide_fusion
  173.8 41.7 %reduce-scatter.2.cloned.1.call-done = bf16[256,1792]{1,0:T(8,128)(2,1)} async-done(((bf16[4096,1792]{1,0:T(8,128)(2,1)}), bf16[256,1792]{1,0:T(8,128)(2,1)}) %reduce-scatter.2.cloned.1.call-update) | async-done | bytes 917520 | tf_op jit(solution)/shard_map/reduce_scatter | solution.py:67
  215.5 3.1 %multiply_convert_fusion = bf16[256,1792]{1,0:T(8,128)(2,1)} fusion(bf16[256,1792]{1,0:T(8,128)(2,1)} %reduce-scatter.2.cloned.1.call-done, s32[256,1792]{1,0:T(8,128)} %param.12), kind=kLoop, calls=%fused_computation.25 | loop fusion | flops 1835008 | bytes 3670016 | tf_op jit(solution)/shard_map/convert_element_type | solution.py:75
  218.6 2.9 %fusion.4 = bf16[256,1792]{1,0:T(8,128)(2,1)} fusion(bf16[256,1792]{1,0:T(8,128)(2,1)} %collective-permute-done.2, bf16[256,1792]{1,0:T(8,128)(2,1)S(1)} %copy-done.6, pred[]{:T(512)S(6)} %eq.35, pred[]{:T(512)S(6)} %eq.34, f32[256,1792]{1,0:T(8,128)S(1)} %copy-done.4, bf16[256,1792]{1,0:T(8,128)(2,1)S(1)} %collective-permute-done, pred[]{:T(512)S(6)} %eq.36), kind=kLoop, calls=%fused_computation.17 | loop fusion | flops 6422528 | bytes 5505027 | tf_op jit(solution)/shard_map/convert_element_type | solution.py:62
  (30 shorter events, 0.4 us)
Async XLA Ops:
  7.2 1.6 copy-start
  7.2 97.1 %all-gather.2.cloned.1.call-start = ((), (), s32[]{:S(2)}) async-start(), calls=%async_computation.1 | async-start | bytes 15597568 | tf_op jit(solution)/shard_map/all_gather | solution.py:58
  7.9 207.6 %reduce-scatter.2.cloned.1.call-start = ((), (), s32[]{:S(2)}) async-start(), calls=%async_computation.2 | async-start | bytes 15597568 | tf_op jit(solution)/shard_map/reduce_scatter | solution.py:67
  26.3 22.5 %collective-permute-start.3 = (bf16[256,1792]{1,0:T(8,128)(2,1)}, bf16[256,1792]{1,0:T(8,128)(2,1)S(1)}, u32[]{:S(2)}, u32[]{:S(2)}) collective-permute-start(bf16[256,1792]{1,0:T(8,128)(2,1)} %convert_element_type.119), channel_id=1, source_target_pairs={{0,1},{1,0},{2,3},{3,2},{4,5},{5,4},{6,7},{7,6},{8,9},{9,8},{10,11... | collective-permute-start | bytes 2752520 | tf_op jit(solution)/shard_map/ppermute | solution.py:14
  51.5 23.5 %collective-permute-start.4 = (bf16[256,1792]{1,0:T(8,128)(2,1)}, bf16[256,1792]{1,0:T(8,128)(2,1)}, u32[]{:S(2)}, u32[]{:S(2)}) collective-permute-start(bf16[256,1792]{1,0:T(8,128)(2,1)} %fusion.14), channel_id=1, source_target_pairs={{0,2},{1,3},{2,0},{3,1},{4,6},{5,7},{6,4},{7,5},{8,10},{9,11},{10,... | collective-permute-start | bytes 2752520 | tf_op jit(solution)/shard_map/ppermute | solution.py:14
  78.3 33.9 %collective-permute-start.5 = (bf16[256,1792]{1,0:T(8,128)(2,1)}, bf16[256,1792]{1,0:T(8,128)(2,1)}, u32[]{:S(2)}, u32[]{:S(2)}) collective-permute-start(bf16[256,1792]{1,0:T(8,128)(2,1)} %fusion.12), channel_id=1, source_target_pairs={{0,4},{1,5},{2,6},{3,7},{4,0},{5,1},{6,2},{7,3},{8,12},{9,13},{10,... | collective-permute-start | bytes 2752520 | tf_op jit(solution)/shard_map/ppermute | solution.py:14
  104.3 8.0 %copy-start.2 = (f32[256,1792]{1,0:T(8,128)S(1)}, f32[256,1792]{1,0:T(8,128)}, u32[]{:S(2)}) copy-start(f32[256,1792]{1,0:T(8,128)} %copy.21) | copy-start | bytes 5505028
  104.3 8.0 %copy-start.7 = (bf16[256,1792]{1,0:T(8,128)(2,1)S(1)}, bf16[256,1792]{1,0:T(8,128)(2,1)}, u32[]{:S(2)}) copy-start(bf16[256,1792]{1,0:T(8,128)(2,1)} %param.8) | copy-start | bytes 2752516
  104.3 8.0 %copy-start.8 = (s32[256,1792]{1,0:T(8,128)S(1)}, s32[256,1792]{1,0:T(8,128)}, u32[]{:S(2)}) copy-start(s32[256,1792]{1,0:T(8,128)} %param.10) | copy-start | bytes 5505028
  122.8 46.3 %copy-start.3 = (f32[256,1792]{1,0:T(8,128)}, f32[256,1792]{1,0:T(8,128)S(1)}, u32[]{:S(2)}) copy-start(f32[256,1792]{1,0:T(8,128)S(1)} %copy.16) | copy-start | bytes 5505028
  122.9 22.6 %collective-permute-start = (bf16[256,1792]{1,0:T(8,128)(2,1)S(1)}, bf16[256,1792]{1,0:T(8,128)(2,1)S(1)}, u32[]{:S(2)}, u32[]{:S(2)}) collective-permute-start(bf16[256,1792]{1,0:T(8,128)(2,1)S(1)} %convert_element_type.110), channel_id=1, source_target_pairs={{0,1},{1,0},{2,3},{3,2},{4,5},{5,4},{6,7},{7,6},{8,9},{9,8},{10,11... | collective-permute-start | bytes 2752520 | tf_op jit(solution)/shard_map/ppermute | solution.py:14
  145.8 23.4 %collective-permute-start.1 = (bf16[256,1792]{1,0:T(8,128)(2,1)S(1)}, bf16[256,1792]{1,0:T(8,128)(2,1)S(1)}, u32[]{:S(2)}, u32[]{:S(2)}) collective-permute-start(bf16[256,1792]{1,0:T(8,128)(2,1)S(1)} %fusion.15), channel_id=1, source_target_pairs={{0,2},{1,3},{2,0},{3,1},{4,6},{5,7},{6,4},{7,5},{8,10},{9,11},{10,... | collective-permute-start | bytes 2752520 | tf_op jit(solution)/shard_map/ppermute | solution.py:14
  169.2 1.5 copy-start.5
  170.6 48.0 %collective-permute-start.2 = (bf16[256,1792]{1,0:T(8,128)(2,1)}, bf16[256,1792]{1,0:T(8,128)(2,1)}, u32[]{:S(2)}, u32[]{:S(2)}) collective-permute-start(bf16[256,1792]{1,0:T(8,128)(2,1)} %fusion.13), channel_id=1, source_target_pairs={{0,4},{1,5},{2,6},{3,7},{4,0},{5,1},{6,2},{7,3},{8,12},{9,13},{10,... | collective-permute-start | bytes 2752520 | tf_op jit(solution)/shard_map/ppermute | solution.py:14
  172.5 0.7 copy-start.9
  215.5 3.1 %copy-start.4 = (f32[256,1792]{1,0:T(8,128)S(1)}, f32[256,1792]{1,0:T(8,128)}, u32[]{:S(2)}) copy-start(f32[256,1792]{1,0:T(8,128)} %copy-done.3) | copy-start | bytes 5505028
  215.5 3.1 %copy-start.6 = (bf16[256,1792]{1,0:T(8,128)(2,1)S(1)}, bf16[256,1792]{1,0:T(8,128)(2,1)}, u32[]{:S(2)}) copy-start(bf16[256,1792]{1,0:T(8,128)(2,1)} %copy-done.5) | copy-start | bytes 2752516
  215.5 6.0 %copy-start.1 = (bf16[256,4096]{1,0:T(8,128)(2,1)S(1)}, bf16[256,4096]{1,0:T(8,128)(2,1)}, u32[]{:S(2)}) copy-start(bf16[256,4096]{1,0:T(8,128)(2,1)} %param.13) | copy-start | bytes 6291460
Sparse Core Ops, SparseCore 0:
  9.7 94.4 all-gather.1
  106.7 108.8 reduce-scatter.1
where the time goes:
time: 229 us; the launch traced here: 228 us
  waiting for transfers between devices  150 us (66%)
  other arithmetic  21.6 us (9%)
  matrix products  20.5 us (9%)
  between operations  14.2 us (6%)
  local copies, waits for them, and re-layouts  11.7 us (5%)
  starting transfers between devices  10.7 us (5%)
    ppermute x6, waiting for transfers between devices, partner_2(): return lax.ppermute(value, axis, pairs)  81.9 us
    reduce_scatter x1, waiting for transfers between devices, shards(): lax.psum_scatter(lax.dot_general(columns, quant_act, (((0,), (0,)), ((),...  41.7 us
    all_gather x1, waiting for transfers between devices, shards(): lax.all_gather(quant_weight, 'dp', axis=0, tiled=True)  25.4 us
    ppermute x6, starting transfers between devices, partner_2(): return lax.ppermute(value, axis, pairs)  10.6 us
    convert_element_type x6, other arithmetic, cross_mix(): values.astype(jnp.bfloat16)  10.4 us
    dot_general x1, matrix products, shards(): lax.dot_general(columns, quant_act, (((0,), (0,)), ((), ())), preferred_e...  8.53 us
    dot_general x1, matrix products, shards(): jnp.dot(columns, lax.all_gather(quant_weight, 'dp', axis=0, tiled=True),...  7.94 us
  transfers between devices with their start and end apart: 8, of which 6 were waited for; matrix products, arithmetic and copies ran while one was open for 22% of the time, Pallas kernels for 0%

commit v1 on v0

v1 whole, which is shorter than its diff:
```python
import functools

import jax
import jax.numpy as jnp
from jax import lax
from jax.experimental import pallas as pl
from jax.experimental.pallas import tpu as pltpu
from jax.sharding import PartitionSpec as P

TB = 256
NH = 896
KB = 256
GROUP = 128
QT = 64
GH = NH // GROUP
MESH = pl.DeviceIdType.MESH
F32 = jnp.float32
BF16 = jnp.bfloat16
KPOS = {0: 0, 1: 1, 3: 2, 2: 3}


def kslot(xo, ry):
    return (xo * 4 + KPOS[ry]) * KB


def rslot(xo, co):
    return (xo * 2 + co) * TB


def group_sums(values, table):
    high = values.astype(BF16)
    low = (values - high.astype(F32)).astype(BF16)
    return jnp.dot(high, table, preferred_element_type=F32) + jnp.dot(low, table, preferred_element_type=F32)


def hadamard4(v0, v1, v2, v3):
    a, b, c, d = v0 + v1, v0 - v1, v2 + v3, v2 - v3
    return a + c, b + d, a - c, b - d


def kernel(
    act, qa, scale, mask, w, wmask, go,
    out_act, out_scale, out_weight,
    go_buf, w_buf, qa_buf, qa_oth, mask_v, wmask_v, a_recv, a_mix, gq_acc, gq_send, gq_recv, gqx_send, gqx_recv,
    g_v, g_recv, o_send, t1, s_send, s_recv, rs_send, rs_recv, dw_own, dwx_send, dwx_recv, dw_out, signs, table,
    send_sems, recv_sems, local_sems,
):
    d = lax.axis_index("dp")
    n = lax.axis_index("tensor")
    X, Y, C = d // 8, (d // 2) % 4, d % 2
    h, z = n // 4, n % 4

    def at(x, y, c):
        return ((x * 4 + y) * 2 + c, n)

    def member(delta):
        return (n + delta) % 8

    sibling = at(X, Y, 1 - C)
    x_side = at(1 - X, Y, C)
    y_up, y_down = at(X, (Y + 1) % 4, C), at(X, (Y + 3) % 4, C)
    z_up, z_down = (d, h * 4 + (z + 1) % 4), (d, h * 4 + (z + 3) % 4)
    own = pl.ds(pl.multiple_of(X * NH, 128), NH)
    oth = pl.ds(pl.multiple_of((1 - X) * NH, 128), NH)
    cols = (own, oth)

    started = []
    count = [0, 0]

    def remote(src, dst, device):
        i = count[0]
        count[0] += 1
        copy = pltpu.make_async_remote_copy(
            src_ref=src, dst_ref=dst, send_sem=send_sems.at[i], recv_sem=recv_sems.at[i], device_id=device, device_id_type=MESH
        )
        copy.start()
        started.append(copy)
        return copy

    def local(src, dst):
        i = count[1]
        count[1] += 1
        copy = pltpu.make_async_copy(src, dst, local_sems.at[i])
        copy.start()
        return copy

    def slice_rows(zz):
        return pl.ds(pl.multiple_of(zz * QT, QT), QT)

    barrier = pltpu.get_barrier_semaphore()
    partners = [sibling, x_side, y_up, y_down] + [(d, member(delta)) for delta in range(1, 8)]
    for partner in partners:
        pl.semaphore_signal(barrier, inc=1, device_id=partner, device_id_type=MESH)

    def k_columns(xo, ry, c):
        x = X if xo == 0 else 1 - X
        return pl.ds(pl.multiple_of(((x * 4 + (Y + ry) % 4) * 2 + c) * KB, KB), KB)

    blocks = [(xo, ry) for xo in (0, 1) for ry in (0, 1, 3, 2)]
    go_own = [local(go.at[:, k_columns(xo, ry, C)], go_buf.at[pl.ds(rslot(0, 0), TB), pl.ds(kslot(xo, ry), KB)]) for xo, ry in blocks]
    w_own = local(w.at[:, own], w_buf.at[pl.ds(kslot(0, 0), KB)])
    qa_own = local(qa.at[:, own], qa_buf.at[pl.ds(rslot(0, 0), TB)])
    qa_oth_in = local(qa.at[:, oth], qa_oth)
    a_own = [local(act.at[slice_rows(z), cols[hf]], a_recv.at[z, hf]) for hf in (0, 1)]
    mask_in = [local(mask.at[:, cols[hf]], mask_v.at[hf]) for hf in (0, 1)]
    wmask_in = [local(wmask.at[:, cols[hf]], wmask_v.at[hf]) for hf in (0, 1)]
    pl.semaphore_wait(barrier, len(partners))

    w_x = remote(w.at[:, oth], w_buf.at[pl.ds(kslot(1, 0), KB)], x_side)
    w_up = [remote(w.at[:, own], w_buf.at[pl.ds(kslot(0, 3), KB)], y_up), None]
    w_down = [remote(w.at[:, own], w_buf.at[pl.ds(kslot(0, 1), KB)], y_down), None]
    go_sib = [
        remote(go.at[:, k_columns(xo, ry, 1 - C)], go_buf.at[pl.ds(rslot(0, 1), TB), pl.ds(kslot(xo, ry), KB)], sibling)
        for xo, ry in blocks
    ]
    a_in = [
        remote(act.at[slice_rows((z + delta) % 4), cols[hf]], a_recv.at[z, hf], (d, h * 4 + (z + delta) % 4))
        for delta in (1, 2, 3)
        for hf in (0, 1)
    ]
    qa_sib = remote(qa.at[:, own], qa_buf.at[pl.ds(rslot(0, 1), TB)], sibling)

    bits = lax.broadcasted_iota(jnp.int32, (GROUP, GROUP), 0) & lax.broadcasted_iota(jnp.int32, (GROUP, GROUP), 1)
    bits = bits ^ (bits >> 4)
    bits = bits ^ (bits >> 2)
    bits = bits ^ (bits >> 1)
    signs[...] = (1 - 2 * (bits & 1)).astype(F32).astype(BF16)
    for hf in (0, 1):
        first = (X if hf == 0 else 1 - X) * GH
        group = lax.broadcasted_iota(jnp.int32, (NH, GROUP), 0) // GROUP + first
        table[hf] = (group == lax.broadcasted_iota(jnp.int32, (NH, GROUP), 1)).astype(F32).astype(BF16)

    def quarter(xo, co):
        return pl.ds(pl.multiple_of(rslot(xo, co) + z * QT, QT), QT)

    def go_cross(co):
        return [
            remote(
                go_buf.at[quarter(0, co), pl.ds(xo * 4 * KB, 4 * KB)],
                go_buf.at[quarter(1, co), pl.ds((1 - xo) * 4 * KB, 4 * KB)],
                x_side,
            )
            for xo in (0, 1)
        ]

    for copy in go_own:
        copy.wait()
    go_x = [go_cross(0), None]
    for copy in go_sib:
        copy.wait_recv()
    go_x[1] = go_cross(1)

    w_x.wait_recv()
    slot = w_buf.at[pl.ds(kslot(1, 0), KB)]
    w_up[1] = remote(slot, w_buf.at[pl.ds(kslot(1, 3), KB)], y_up)
    w_down[1] = remote(slot, w_buf.at[pl.ds(kslot(1, 1), KB)], y_down)
    w_up[0].wait_recv()
    w_far0 = remote(w_buf.at[pl.ds(kslot(0, 3), KB)], w_buf.at[pl.ds(kslot(0, 2), KB)], y_up)

    go_up, go_down = [], []
    for co in (0, 1):
        for copy in go_x[co]:
            copy.wait_recv()
        here = go_buf.at[quarter(1, co)]
        go_up.append(remote(here, here, z_up))
        go_down.append(remote(here, here, z_down))
    qa_x = remote(qa.at[:, oth], qa_buf.at[pl.ds(rslot(1, 0), TB)], x_side)

    for copy in a_own:
        copy.wait()
    for copy in a_in:
        copy.wait_recv()
    for hf in (0, 1):
        mixed = hadamard4(*[a_recv[zz, hf].astype(F32) for zz in range(4)])
        for zz in range(4):
            a_mix[zz, hf] = mixed[zz]

    w_down[1].wait_recv()
    w_far1 = remote(w_buf.at[pl.ds(kslot(1, 1), KB)], w_buf.at[pl.ds(kslot(1, 2), KB)], y_down)

    def quarter_of(zz, co):
        return pl.ds(pl.multiple_of(rslot(1, co) + (zz % 4) * QT, QT), QT)

    go_up[0].wait_recv()
    passed = go_buf.at[quarter_of(z + 3, 0)]
    go_far0 = remote(passed, passed, z_up)
    go_down[1].wait_recv()
    passed = go_buf.at[quarter_of(z + 1, 1)]
    go_far1 = remote(passed, passed, z_down)

    qa_x.wait_recv()
    qa_far = remote(qa_buf.at[pl.ds(rslot(1, 0), TB)], qa_buf.at[pl.ds(rslot(1, 1), TB)], sibling)

    w_own.wait()
    w_down[0].wait_recv()
    w_up[1].wait_recv()
    w_far0.wait_recv()
    w_far1.wait_recv()
    go_down[0].wait_recv()
    go_up[1].wait_recv()
    go_far0.wait_recv()
    go_far1.wait_recv()
    qa_own.wait()
    qa_sib.wait_recv()
    qa_far.wait_recv()

    def weight_block(xo, ry):
        return lax.dot_general(
            go_buf[:, kslot(xo, ry) : kslot(xo, ry) + KB], qa_buf[...], (((0,), (0,)), ((), ())), preferred_element_type=F32
        )

    rs_send[0] = weight_block(0, 2).astype(BF16)
    rs_far0 = remote(rs_send.at[0], rs_recv.at[0], y_up)
    rs_send[1] = weight_block(1, 2).astype(BF16)
    rs_far1 = remote(rs_send.at[1], rs_recv.at[1], y_down)

    def quant_rows(xo, co):
        return jnp.dot(go_buf[rslot(xo, co) : rslot(xo, co) + TB], w_buf[...], preferred_element_type=F32)

    gq_sib = [None, None]
    for xo in (1, 0):
        gq_send[xo] = quant_rows(xo, 1).astype(BF16)
        gq_sib[xo] = remote(gq_send.at[xo], gq_recv.at[xo], sibling)
    for xo in (1, 0):
        gq_acc[xo] = quant_rows(xo, 0)
    gq_sib[1].wait_recv()
    gqx_send[...] = (gq_acc[1] + gq_recv[1].astype(F32)).astype(BF16)
    gq_x = remote(gqx_send, gqx_recv, x_side)

    for copy in mask_in:
        copy.wait()
    qa_oth_in.wait()

    def rotate_half(hf, quant, quantized):
        wide = quant.astype(F32)
        sums = group_sums(wide * quantized.astype(F32), table[hf])
        if hf == 0:
            t1[...] = sums
        else:
            t1[...] += sums
        rot = (wide * mask_v[hf].astype(F32)).astype(BF16)
        for g in range(GH):
            part = slice(g * GROUP, (g + 1) * GROUP)
            g_v[hf, :, part] = jnp.dot(rot[:, part], signs[...], preferred_element_type=F32).astype(BF16)
        copies = []
        for delta in range(1, 8):
            to = member(delta)
            copies.append(remote(g_v.at[hf, slice_rows(to % 4)], g_recv.at[n, hf], (d, to)))
        return copies, local(g_v.at[hf, slice_rows(z)], g_recv.at[n, hf])

    gq_sib[0].wait_recv()
    g_in = [None, None]
    g_in[0] = rotate_half(0, (gq_acc[0] + gq_recv[0].astype(F32)).astype(BF16), qa_buf[0:TB])

    rs_send[2] = weight_block(1, 1).astype(BF16)
    rs_near_up1 = remote(rs_send.at[2], rs_recv.at[2], y_up)
    rs_send[3] = weight_block(0, 3).astype(BF16)
    rs_near_down0 = remote(rs_send.at[3], rs_recv.at[3], y_down)
    for xo in (0, 1):
        dw_own[xo] = weight_block(xo, 0)
    dw_own[2] = weight_block(0, 1)
    dw_own[3] = weight_block(1, 3)
    rs_far0.wait_recv()
    rs_send[4] = (dw_own[2] + rs_recv[0].astype(F32)).astype(BF16)
    rs_near_up0 = remote(rs_send.at[4], rs_recv.at[4], y_up)
    rs_far1.wait_recv()
    rs_send[5] = (dw_own[3] + rs_recv[1].astype(F32)).astype(BF16)
    rs_near_down1 = remote(rs_send.at[5], rs_recv.at[5], y_down)

    gq_x.wait_recv()
    g_in[1] = rotate_half(1, gqx_recv[...], qa_oth[...])

    sign = (1 - 2 * h).astype(F32)

    def mix_half(hf):
        copies, kept = g_in[hf]
        for copy in copies:
            copy.wait_recv()
        kept.wait()
        sums = []
        for zz in range(4):
            low, high = g_recv[zz, hf].astype(F32), g_recv[4 + zz, hf].astype(F32)
            sums.append(low + sign * high)
            for hh, value in ((0, low), (1, sign * high)):
                part = group_sums(value * a_mix[zz, hf], table[hf])
                if hf == 0:
                    s_send[hh * 4 + zz] = part
                else:
                    s_send[hh * 4 + zz] += part
        mixed = hadamard4(*sums)
        for zz in range(4):
            o_send[zz, hf] = (mixed[zz] * (1.0 / 32.0)).astype(BF16)
        copies = []
        for delta in (1, 2, 3):
            to = (z + delta) % 4
            copies.append(remote(o_send.at[to, hf], out_act.at[slice_rows(z), cols[hf]], (d, h * 4 + to)))
        return copies, local(o_send.at[z, hf], out_act.at[slice_rows(z), cols[hf]])

    o_in = [mix_half(0), None]

    rs_near_up1.wait_recv()
    rs_near_down1.wait_recv()
    dwx_send[...] = (dw_own[1] + rs_recv[2].astype(F32) + rs_recv[5].astype(F32)).astype(BF16)
    dw_x = remote(dwx_send, dwx_recv, x_side)
    rs_near_up0.wait_recv()
    rs_near_down0.wait_recv()
    for copy in wmask_in:
        copy.wait()
    dw_out[0] = ((dw_own[0] + rs_recv[3].astype(F32) + rs_recv[4].astype(F32)) * wmask_v[0].astype(F32)).astype(BF16)
    dw_done = [local(dw_out.at[0], out_weight.at[:, own]), None]

    o_in[1] = mix_half(1)
    s_in = [remote(s_send.at[member(delta)], s_recv.at[n], (d, member(delta))) for delta in range(1, 8)]
    s_kept = local(s_send.at[n], s_recv.at[n])

    dw_x.wait_recv()
    dw_out[1] = (dwx_recv[...].astype(F32) * wmask_v[1].astype(F32)).astype(BF16)
    dw_done[1] = local(dw_out.at[1], out_weight.at[:, oth])

    for copy in s_in:
        copy.wait_recv()
    s_kept.wait()
    for zz in range(4):
        rows = slice(zz * QT, (zz + 1) * QT)
        total = t1[rows] - (s_recv[zz] + s_recv[4 + zz]) * (1.0 / 32.0)
        out_scale[rows] = total[:, : 2 * GH] / (scale[rows] * (7.0 * GROUP) ** 0.5)

    for copies, kept in o_in:
        for copy in copies:
            copy.wait_recv()
        kept.wait()
    for copy in dw_done:
        copy.wait()
    for copy in started:
        copy.wait_send()


def shards(activations, quant_act, act_scale, act_mask, quant_weight, weight_mask, grad_out):
    anywhere = pl.BlockSpec(memory_space=pl.ANY)
    vmem = pl.BlockSpec(memory_space=pltpu.VMEM)
    half = (TB, NH)
    return pl.pallas_call(
        kernel,
        out_shape=(
            jax.ShapeDtypeStruct((TB, 2 * NH), BF16),
            jax.ShapeDtypeStruct((TB, 2 * GH), F32),
            jax.ShapeDtypeStruct((TB, 2 * NH), BF16),
        ),
        in_specs=[anywhere, anywhere, vmem, anywhere, anywhere, anywhere, anywhere],
        out_specs=(anywhere, vmem, anywhere),
        scratch_shapes=[
            pltpu.VMEM((4 * TB, 8 * KB), BF16),
            pltpu.VMEM((8 * KB, NH), BF16),
            pltpu.VMEM((4 * TB, NH), BF16),
            pltpu.VMEM(half, BF16),
            pltpu.VMEM((2,) + half, jnp.int32),
            pltpu.VMEM((2,) + half, jnp.int32),
            pltpu.VMEM((4, 2, QT, NH), BF16),
            pltpu.VMEM((4, 2, QT, NH), F32),
            pltpu.VMEM((2,) + half, F32),
            pltpu.VMEM((2,) + half, BF16),
            pltpu.VMEM((2,) + half, BF16),
            pltpu.VMEM(half, BF16),
            pltpu.VMEM(half, BF16),
            pltpu.VMEM((2,) + half, BF16),
            pltpu.VMEM((8, 2, QT, NH), BF16),
            pltpu.VMEM((4, 2, QT, NH), BF16),
            pltpu.VMEM((TB, GROUP), F32),
            pltpu.VMEM((8, QT, GROUP), F32),
            pltpu.VMEM((8, QT, GROUP), F32),
            pltpu.VMEM((6,) + half, BF16),
            pltpu.VMEM((6,) + half, BF16),
            pltpu.VMEM((4,) + half, F32),
            pltpu.VMEM(half, BF16),
            pltpu.VMEM(half, BF16),
            pltpu.VMEM((2,) + half, BF16),
            pltpu.VMEM((GROUP, GROUP), BF16),
            pltpu.VMEM((2, NH, GROUP), BF16),
            pltpu.SemaphoreType.DMA((72,)),
            pltpu.SemaphoreType.DMA((72,)),
            pltpu.SemaphoreType.DMA((32,)),
        ],
        compiler_params=pltpu.CompilerParams(collective_id=0, has_side_effects=True, vmem_limit_bytes=56 * 2**20),
        cost_estimate=pl.CostEstimate(flops=7516192768, bytes_accessed=16 * 2**20, transcendentals=0),
    )(activations, quant_act, act_scale, act_mask, quant_weight, weight_mask, grad_out)


def solution(mesh):
    return jax.shard_map(
        shards,
        mesh=mesh,
        in_specs=(
            P("dp", "tensor"),
            P("dp", "tensor"),
            P("dp", "tensor"),
            P("dp", "tensor"),
            P("dp", "tensor"),
            P("dp", "tensor"),
            P("dp", None),
        ),
        out_specs=(P("dp", "tensor"), P("dp", "tensor"), P("dp", "tensor")),
        check_vma=False,
    )
```

time: 229 us -> 106 us (0.46)
  waiting for transfers between devices: 150 us -> 0 us
  Pallas kernels: 0 us -> 98.7 us
  other arithmetic: 21.6 us -> 0 us
  matrix products: 20.5 us -> 0 us
  between operations: 14.2 us -> 0.65 us
  starting transfers between devices: 10.7 us -> 0 us
  local copies, waits for them, and re-layouts: 11.7 us -> 6.24 us
    pallas_call x0 -> x1, Pallas kernels: none -> 98.7 us  [shards(): pl.pallas_call(kernel, out_shape=(jax.ShapeDtypeStruct((TB, 2 * NH), BF16...]
    ppermute x6 -> x0, waiting for transfers between devices: 81.9 us -> none  [partner_2(): return lax.ppermute(value, axis, pairs)]
    reduce_scatter x1 -> x0, waiting for transfers between devices: 41.7 us -> none  [shards(): lax.psum_scatter(lax.dot_general(columns, quant_act, (((0,), (0,)), ((),...]
    all_gather x1 -> x0, waiting for transfers between devices: 25.4 us -> none  [shards(): lax.all_gather(quant_weight, 'dp', axis=0, tiled=True)]
    dot_general x4 -> x0, matrix products: 20.5 us -> none  [the longest x1 8.53 us: shards(): lax.dot_general(columns, quant_act, (((0,), (0,)), ((), ())), preferred_e...]
    convert_element_type x8 -> x0, other arithmetic: 16.4 us -> none  [the longest x6 10.4 us: cross_mix(): values.astype(jnp.bfloat16)]
    ppermute x6 -> x0, starting transfers between devices: 10.6 us -> none  [partner_2(): return lax.ppermute(value, axis, pairs)]
    mul x4 -> x0, local copies, waits for them, and re-layouts: 8.81 us -> none  [the longest x1 3.2 us: local_mix_narrow(): return mixed.reshape(rows, width) * (1.0 / math.sqrt(GROUP))]
  transfers between devices with their start and end apart: 8 -> 0, of which waited for: 6 -> 0; matrix products, arithmetic and copies ran while one was open for 22% -> 0% of each run, Pallas kernels for 0% -> 0%
where the time goes in v1:
time: 106 us
  Pallas kernels  98.7 us (93%)
  local copies, waits for them, and re-layouts  6.24 us (6%)
    pallas_call x1, Pallas kernels, shards(): pl.pallas_call(kernel, out_shape=(jax.ShapeDtypeStruct((TB, 2 * NH), BF16...  98.7 us
    unnamed x5, local copies, waits for them, and re-layouts  4.57 us

profile of v1, /device:TPU:4, one launch (start us, length us, event | category | flops | bytes accessed | tf_op | source)
XLA Modules:
  0.0 105.6 jit_solution(1153241084032842353)
XLA Ops:
  0.6 1.5 %copy.10.scale = f32[256,14]{1,0:T(8,128)} copy(f32[256,14]{0,1:T(8,128)} %param.9) | data formatting | bytes 28672 | tf_op args[2]
  2.1 98.7 %shard_map.94 = (bf16[256,1792]{1,0:T(8,128)(2,1)}, f32[256,14]{1,0:T(8,128)}, bf16[256,1792]{1,0:T(8,128)(2,1)}) custom-call(bf16[256,1792]{1,0:T(8,128)(2,1)} %act.1, bf16[256,1792]{1,0:T(8,128)(2,1)} %qa.1, f32[256,14]{1,0:T(8,128)} %copy.10.scale, s32[256,1792]{1,0:T(8,128)} %mask.1, bf16[256,1792]{1,0:T(8,128)(2,1)} %w.1, s32[256,1792]{1,0:T(8,128)} %wmask.1, ...), custom_call_target="tpu_custom_call" | custom-call | flops 7516192768 | bytes 16777216 | tf_op jit(solution)/shard_map/pallas_call | solution.py:342
  100.8 0.0 copy-start
  100.8 1.7 %copy.11 = f32[256,14]{0,1:T(8,128)} copy(f32[256,14]{1,0:T(8,128)} %get-tuple-element.4) | data formatting | bytes 28672 | tf_op jit(solution)/shard_map/pallas_call | solution.py:342
  102.5 2.2 %copy.14 = bf16[256,1792]{1,0:T(8,128)(2,1)} copy(bf16[256,1792]{1,0:T(8,128)(2,1)} %get-tuple-element.9) | data formatting | bytes 1835008
  104.6 0.0 copy-done
  104.6 0.9 copy.15
Async XLA Ops:
  100.8 3.8 %copy-start = (bf16[256,1792]{1,0:T(8,128)(2,1)S(1)}, bf16[256,1792]{1,0:T(8,128)(2,1)}, u32[]{:S(2)}) copy-start(bf16[256,1792]{1,0:T(8,128)(2,1)} %get-tuple-element.11) | copy-start | bytes 2752516

commit v2 on v1

v2 whole, which is shorter than its diff:
```python
import functools

import jax
import jax.numpy as jnp
from jax import lax
from jax.experimental import pallas as pl
from jax.experimental.pallas import tpu as pltpu
from jax.sharding import PartitionSpec as P

TB = 256
NH = 896
KB = 256
HB = 128
GROUP = 128
QT = 64
GH = NH // GROUP
CHUNKS = ((0, 256), (256, 256), (512, 384))
MESH = pl.DeviceIdType.MESH
F32 = jnp.float32
BF16 = jnp.bfloat16
KPOS = {0: 0, 1: 1, 3: 2, 2: 3}


def kslot(xo, ry):
    return (xo * 4 + KPOS[ry]) * KB


def rslot(xo, co):
    return (xo * 2 + co) * TB


def group_sums(values, table):
    high = values.astype(BF16)
    low = (values - high.astype(F32)).astype(BF16)
    return jnp.dot(high, table, preferred_element_type=F32) + jnp.dot(low, table, preferred_element_type=F32)


def hadamard4(v0, v1, v2, v3):
    a, b, c, d = v0 + v1, v0 - v1, v2 + v3, v2 - v3
    return a + c, b + d, a - c, b - d


def kernel(
    act, qa, scale, mask, w, wmask, go,
    out_act, out_scale, out_weight,
    go_buf, w_buf, qa_buf, qa_oth, mask_v, wmask_v, a_recv, a_mix, gq_part, gq_send, gq_recv, gqx_send, gqx_recv,
    g_v, g_recv, o_send, t1, p_v, s_send, s_recv, rs_send, rs_recv, dw_own, dw_near, dwx_send, dwx_recv, dw_out, signs, table,
    send_sems, recv_sems, local_sems,
):
    d = lax.axis_index("dp")
    n = lax.axis_index("tensor")
    X, Y, C = d // 8, (d // 2) % 4, d % 2
    h, z = n // 4, n % 4

    def at(x, y, c):
        return ((x * 4 + y) * 2 + c, n)

    def member(delta):
        return (n + delta) % 8

    sibling = at(X, Y, 1 - C)
    x_side = at(1 - X, Y, C)
    x_across = (((1 - X) * 4 + Y) * 2 + C, (n + 4) % 8)
    y_up, y_down = at(X, (Y + 1) % 4, C), at(X, (Y + 3) % 4, C)
    z_up, z_down = (d, h * 4 + (z + 1) % 4), (d, h * 4 + (z + 3) % 4)
    own = pl.ds(pl.multiple_of(X * NH, 128), NH)
    oth = pl.ds(pl.multiple_of((1 - X) * NH, 128), NH)
    cols = (own, oth)

    def columns(hf, c):
        base = (X if hf == 0 else 1 - X) * NH
        return pl.ds(pl.multiple_of(base + CHUNKS[c][0], 128), CHUNKS[c][1])

    started = []
    count = [0, 0]

    def remote(src, dst, device):
        i = count[0]
        count[0] += 1
        copy = pltpu.make_async_remote_copy(
            src_ref=src, dst_ref=dst, send_sem=send_sems.at[i], recv_sem=recv_sems.at[i], device_id=device, device_id_type=MESH
        )
        copy.start()
        started.append(copy)
        return copy

    def local(src, dst):
        i = count[1]
        count[1] += 1
        copy = pltpu.make_async_copy(src, dst, local_sems.at[i])
        copy.start()
        return copy

    def slice_rows(zz):
        return pl.ds(pl.multiple_of(zz * QT, QT), QT)

    barrier = pltpu.get_barrier_semaphore()
    partners = [sibling, x_side, x_across, y_up, y_down] + [(d, member(delta)) for delta in range(1, 8)]
    for partner in partners:
        pl.semaphore_signal(barrier, inc=1, device_id=partner, device_id_type=MESH)

    def k_columns(xo, ry, c):
        x = X if xo == 0 else 1 - X
        return pl.ds(pl.multiple_of(((x * 4 + (Y + ry) % 4) * 2 + c) * KB, KB), KB)

    blocks = [(xo, ry) for xo in (0, 1) for ry in (0, 1, 3, 2)]
    go_own = [local(go.at[:, k_columns(xo, ry, C)], go_buf.at[pl.ds(rslot(0, 0), TB), pl.ds(kslot(xo, ry), KB)]) for xo, ry in blocks]
    w_own = local(w.at[:, own], w_buf.at[pl.ds(kslot(0, 0), KB)])
    qa_own = local(qa.at[:, own], qa_buf.at[pl.ds(rslot(0, 0), TB)])
    qa_oth_in = local(qa.at[:, oth], qa_oth)
    a_own = [local(act.at[slice_rows(z), cols[hf]], a_recv.at[z, hf]) for hf in (0, 1)]
    mask_in = [local(mask.at[:, cols[hf]], mask_v.at[hf]) for hf in (0, 1)]
    wmask_in = [local(wmask.at[:, cols[hf]], wmask_v.at[hf]) for hf in (0, 1)]
    pl.semaphore_wait(barrier, len(partners))

    def inner(c):
        return pl.ds(*CHUNKS[c])

    def w_cross(c):
        return remote(w.at[:, columns(1, c)], w_buf.at[pl.ds(kslot(1, 0), KB), inner(c)], x_side)

    def w_first(c, ry, device):
        return remote(w.at[:, columns(0, c)], w_buf.at[pl.ds(kslot(0, ry), KB), inner(c)], device)

    def w_pass(c, xo, come, go_to, device):
        here = w_buf.at[pl.ds(kslot(xo, come), KB), inner(c)]
        return remote(here, w_buf.at[pl.ds(kslot(xo, go_to), KB), inner(c)], device)

    w_x, w_up0, w_down0, w_up1, w_down1, w_far0, w_far1 = ([None] * 3 for _ in range(7))
    def w_own_pair(c):
        w_up0[c] = w_first(c, 3, y_up)
        w_down0[c] = w_first(c, 1, y_down)

    def w_pass_pair(c):
        w_x[c].wait_recv()
        w_up1[c] = w_pass(c, 1, 0, 3, y_up)
        w_down1[c] = w_pass(c, 1, 0, 1, y_down)

    def w_up_on(c):
        w_up0[c].wait_recv()
        w_far0[c] = w_pass(c, 0, 3, 2, y_up)

    def w_down_on(c):
        w_down1[c].wait_recv()
        w_far1[c] = w_pass(c, 1, 1, 2, y_down)

    def w_complete(c):
        for copy in (w_down0[c], w_up1[c], w_far0[c], w_far1[c]):
            copy.wait_recv()

    w_x[0] = w_cross(0)
    w_own_pair(0)
    go_sib = [
        remote(go.at[:, k_columns(xo, ry, 1 - C)], go_buf.at[pl.ds(rslot(0, 1), TB), pl.ds(kslot(xo, ry), KB)], sibling)
        for xo, ry in blocks
    ]
    a_in = [
        remote(act.at[slice_rows((z + delta) % 4), cols[hf]], a_recv.at[z, hf], (d, h * 4 + (z + delta) % 4))
        for delta in (1, 2, 3)
        for hf in (0, 1)
    ]
    qa_sib = remote(qa.at[:, own], qa_buf.at[pl.ds(rslot(0, 1), TB)], sibling)

    bits = lax.broadcasted_iota(jnp.int32, (GROUP, GROUP), 0) & lax.broadcasted_iota(jnp.int32, (GROUP, GROUP), 1)
    bits = bits ^ (bits >> 4)
    bits = bits ^ (bits >> 2)
    bits = bits ^ (bits >> 1)
    signs[...] = (1 - 2 * (bits & 1)).astype(F32).astype(BF16)
    for hf in (0, 1):
        first = (X if hf == 0 else 1 - X) * GH
        group = lax.broadcasted_iota(jnp.int32, (NH, GROUP), 0) // GROUP + first
        table[hf] = (group == lax.broadcasted_iota(jnp.int32, (NH, GROUP), 1)).astype(F32).astype(BF16)

    def quarter(xo, co, zz):
        return pl.ds(pl.multiple_of(rslot(xo, co) + (zz % 4) * QT, QT), QT)

    def go_cross(co):
        return [
            remote(
                go_buf.at[quarter(0, co, z), pl.ds(xo * 4 * KB, 4 * KB)],
                go_buf.at[quarter(1, co, z), pl.ds((1 - xo) * 4 * KB, 4 * KB)],
                x_across,
            )
            for xo in (0, 1)
        ]

    def go_along(co):
        for copy in go_x[co]:
            copy.wait_recv()
        here = go_buf.at[quarter(1, co, z)]
        return remote(here, here, z_up), remote(here, here, z_down)

    for copy in go_own:
        copy.wait()
    go_x = [go_cross(0), None]
    w_x[1] = w_cross(1)
    w_own_pair(1)
    for copy in go_sib:
        copy.wait_recv()
    go_x[1] = go_cross(1)
    w_pass_pair(0)
    w_x[2] = w_cross(2)
    w_up_on(0)
    go_up, go_down = [None, None], [None, None]
    go_up[0], go_down[0] = go_along(0)
    w_pass_pair(1)
    qa_x = remote(qa.at[:, oth], qa_buf.at[pl.ds(rslot(1, 0), TB)], x_side)
    w_down_on(0)
    w_up_on(1)
    w_own_pair(2)
    go_up[1], go_down[1] = go_along(1)

    for copy in a_own:
        copy.wait()
    for copy in a_in:
        copy.wait_recv()
    for hf in (0, 1):
        mixed = hadamard4(*[a_recv[zz, hf].astype(F32) for zz in range(4)])
        for zz in range(4):
            a_mix[zz, hf] = mixed[zz]

    w_pass_pair(2)

    def quant_rows(xo, co, c):
        first, width = CHUNKS[c]
        return jnp.dot(
            go_buf[rslot(xo, co) : rslot(xo, co) + TB], w_buf[:, first : first + width], preferred_element_type=F32
        )

    gq_sib = {}

    def quant_start(xo, c):
        part = slice(CHUNKS[c][0], sum(CHUNKS[c]))
        gq_send[xo, :, part] = quant_rows(xo, 1, c).astype(BF16)
        gq_sib[xo, c] = remote(gq_send.at[xo, :, inner(c)], gq_recv.at[xo, :, inner(c)], sibling)
        gq_part[xo, :, part] = quant_rows(xo, 0, c)

    def quant_end(xo, c):
        part = slice(CHUNKS[c][0], sum(CHUNKS[c]))
        gq_sib[xo, c].wait_recv()
        return (gq_part[xo, :, part] + gq_recv[xo, :, part].astype(F32)).astype(BF16)

    gq_x = [None] * 3

    def quant_cross(c):
        part = slice(CHUNKS[c][0], sum(CHUNKS[c]))
        gqx_send[:, part] = quant_end(1, c)
        gq_x[c] = remote(gqx_send.at[:, inner(c)], gqx_recv.at[:, inner(c)], x_side)

    g_in = {}

    def rotate(hf, c, quant):
        first, width = CHUNKS[c]
        part = slice(first, first + width)
        wide = quant.astype(F32)
        rot = (wide * mask_v[hf, :, part].astype(F32)).astype(BF16)
        for g in range(width // GROUP):
            g_v[hf, :, first + g * GROUP : first + (g + 1) * GROUP] = jnp.dot(
                rot[:, g * GROUP : (g + 1) * GROUP], signs[...], preferred_element_type=F32
            ).astype(BF16)
        copies = []
        for delta in range(1, 8):
            to = member(delta)
            copies.append(remote(g_v.at[hf, slice_rows(to % 4), inner(c)], g_recv.at[n, hf, :, inner(c)], (d, to)))
        g_in[hf, c] = copies, local(g_v.at[hf, slice_rows(z), inner(c)], g_recv.at[n, hf, :, inner(c)])
        quantized = qa_buf[0:TB, part] if hf == 0 else qa_oth[:, part]
        sums = group_sums(wide * quantized.astype(F32), table[hf, part])
        if hf == 0 and c == 0:
            t1[...] = sums
        else:
            t1[...] += sums

    def weight_block(xo, ry):
        return lax.dot_general(
            go_buf[:, kslot(xo, ry) : kslot(xo, ry) + KB], qa_buf[...], (((0,), (0,)), ((), ())), preferred_element_type=F32
        )

    rs_far, rs_alone, rs_added = {}, {}, {}

    def reduce_far(xo):
        rs_send[xo, 0] = weight_block(xo, 2).astype(BF16)
        rs_far[xo] = [
            remote(rs_send.at[xo, 0, pl.ds(i * HB, HB)], rs_recv.at[xo, 0, pl.ds(i * HB, HB)], (y_up, y_down)[i]) for i in (0, 1)
        ]

    def reduce_near(xo):
        rs_alone[xo] = []
        for i, ry in ((0, 1), (1, 3)):
            value = weight_block(xo, ry)
            dw_near[xo, i] = value[i * HB : (i + 1) * HB]
            rs_send[xo, 1 + i, (1 - i) * HB : (2 - i) * HB] = value[(1 - i) * HB : (2 - i) * HB].astype(BF16)
            part = pl.ds((1 - i) * HB, HB)
            rs_alone[xo].append(remote(rs_send.at[xo, 1 + i, part], rs_recv.at[xo, 1 + i, part], (y_up, y_down)[i]))

    def reduce_pass(xo):
        rs_added[xo] = []
        for i in (0, 1):
            rs_far[xo][i].wait_recv()
            rows = slice(i * HB, (i + 1) * HB)
            rs_send[xo, 1 + i, rows] = (dw_near[xo, i] + rs_recv[xo, 0, rows].astype(F32)).astype(BF16)
            part = pl.ds(i * HB, HB)
            rs_added[xo].append(remote(rs_send.at[xo, 1 + i, part], rs_recv.at[xo, 1 + i, part], (y_up, y_down)[i]))

    def reduce_end(xo):
        for copy in rs_alone[xo] + rs_added[xo]:
            copy.wait_recv()
        return dw_own[xo] + rs_recv[xo, 1].astype(F32) + rs_recv[xo, 2].astype(F32)

    w_own.wait()
    w_complete(0)
    quant_start(0, 0)
    w_down_on(1)
    go_up[0].wait_recv()
    passed = go_buf.at[quarter(1, 0, z + 3)]
    go_far0 = remote(passed, passed, z_up)
    for copy in mask_in:
        copy.wait()
    qa_own.wait()
    qa_oth_in.wait()
    rotate(0, 0, quant_end(0, 0))
    w_up_on(2)
    go_down[1].wait_recv()
    passed = go_buf.at[quarter(1, 1, z + 1)]
    go_far1 = remote(passed, passed, z_down)
    qa_x.wait_recv()
    qa_far = remote(qa_buf.at[pl.ds(rslot(1, 0), TB)], qa_buf.at[pl.ds(rslot(1, 1), TB)], sibling)
    w_complete(1)
    quant_start(0, 1)
    w_down_on(2)
    rotate(0, 1, quant_end(0, 1))
    for copy in (go_down[0], go_up[1], go_far0, go_far1):
        copy.wait_recv()
    quant_start(1, 0)
    qa_sib.wait_recv()
    qa_far.wait_recv()
    reduce_far(1)
    quant_cross(0)
    quant_start(1, 1)
    reduce_near(1)
    quant_cross(1)
    w_complete(2)
    quant_start(0, 2)
    reduce_far(0)
    rotate(0, 2, quant_end(0, 2))
    quant_start(1, 2)
    reduce_near(0)
    quant_cross(2)
    gq_x[0].wait_recv()
    rotate(1, 0, gqx_recv[:, 0:256])
    reduce_pass(1)
    gq_x[1].wait_recv()
    rotate(1, 1, gqx_recv[:, 256:512])
    reduce_pass(0)
    dw_own[1] = weight_block(1, 0)
    dw_own[0] = weight_block(0, 0)

    sign = (1 - 2 * h).astype(F32)

    o_in = []

    def mix(hf, c):
        first, width = CHUNKS[c]
        part = slice(first, first + width)
        copies, kept = g_in[hf, c]
        for copy in copies:
            copy.wait_recv()
        kept.wait()
        sums = []
        for zz in range(4):
            sums.append(g_recv[zz, hf, :, part].astype(F32) + sign * g_recv[4 + zz, hf, :, part].astype(F32))
        mixed = hadamard4(*sums)
        for zz in range(4):
            o_send[zz, hf, :, part] = (mixed[zz] * (1.0 / 32.0)).astype(BF16)
        copies = []
        for delta in (1, 2, 3):
            to = (z + delta) % 4
            copies.append(remote(o_send.at[to, hf, :, inner(c)], out_act.at[slice_rows(z), columns(hf, c)], (d, h * 4 + to)))
        o_in.append((copies, local(o_send.at[z, hf, :, inner(c)], out_act.at[slice_rows(z), columns(hf, c)])))
        for m in range(8):
            value = g_recv[m, hf, :, part].astype(F32) * a_mix[m % 4, hf, :, part]
            top = value.astype(BF16)
            rows = slice(m * QT, (m + 1) * QT)
            p_v[0, rows, part] = top
            p_v[1, rows, part] = (value - top.astype(F32)).astype(BF16)
        sums = jnp.dot(p_v[0, :, part], table[hf, part], preferred_element_type=F32)
        sums += jnp.dot(p_v[1, :, part], table[hf, part], preferred_element_type=F32)
        if hf == 0 and c == 0:
            s_send[...] = sums
        else:
            s_send[...] += sums

    mix(0, 0)
    gq_x[2].wait_recv()
    rotate(1, 2, gqx_recv[:, 512:896])
    mix(0, 1)
    mix(0, 2)
    dwx_send[...] = reduce_end(1).astype(BF16)
    dw_x = remote(dwx_send, dwx_recv, x_side)
    mix(1, 0)
    mix(1, 1)
    mix(1, 2)
    s_send[4 * QT :] *= sign
    s_in = [
        remote(s_send.at[pl.ds(pl.multiple_of(member(delta) * QT, QT), QT)], s_recv.at[n], (d, member(delta))) for delta in range(1, 8)
    ]
    s_kept = local(s_send.at[pl.ds(pl.multiple_of(n * QT, QT), QT)], s_recv.at[n])

    for copy in wmask_in:
        copy.wait()
    dw_out[0] = (reduce_end(0) * wmask_v[0].astype(F32)).astype(BF16)
    dw_done = [local(dw_out.at[0], out_weight.at[:, own]), None]

    dw_x.wait_recv()
    dw_out[1] = (dwx_recv[...].astype(F32) * wmask_v[1].astype(F32)).astype(BF16)
    dw_done[1] = local(dw_out.at[1], out_weight.at[:, oth])

    for copy in s_in:
        copy.wait_recv()
    s_kept.wait()
    for zz in range(4):
        rows = slice(zz * QT, (zz + 1) * QT)
        t1[rows] -= (s_recv[zz] + s_recv[4 + zz]) * (1.0 / 32.0)
    out_scale[...] = t1[...].T[: 2 * GH] / (scale[...] * (7.0 * GROUP) ** 0.5)

    for copies, kept in o_in:
        for copy in copies:
            copy.wait_recv()
        kept.wait()
    for copy in dw_done:
        copy.wait()
    for copy in started:
        copy.wait_send()


def shards(activations, quant_act, act_scale, act_mask, quant_weight, weight_mask, grad_out):
    anywhere = pl.BlockSpec(memory_space=pl.ANY)
    vmem = pl.BlockSpec(memory_space=pltpu.VMEM)
    half = (TB, NH)
    grad_act, grad_scale, grad_weight = pl.pallas_call(
        kernel,
        out_shape=(
            jax.ShapeDtypeStruct((TB, 2 * NH), BF16),
            jax.ShapeDtypeStruct((2 * GH, TB), F32),
            jax.ShapeDtypeStruct((TB, 2 * NH), BF16),
        ),
        in_specs=[anywhere, anywhere, vmem, anywhere, anywhere, anywhere, anywhere],
        out_specs=(anywhere, vmem, anywhere),
        scratch_shapes=[
            pltpu.VMEM((4 * TB, 8 * KB), BF16),
            pltpu.VMEM((8 * KB, NH), BF16),
            pltpu.VMEM((4 * TB, NH), BF16),
            pltpu.VMEM(half, BF16),
            pltpu.VMEM((2,) + half, jnp.int32),
            pltpu.VMEM((2,) + half, jnp.int32),
            pltpu.VMEM((4, 2, QT, NH), BF16),
            pltpu.VMEM((4, 2, QT, NH), F32),
            pltpu.VMEM((2,) + half, F32),
            pltpu.VMEM((2,) + half, BF16),
            pltpu.VMEM((2,) + half, BF16),
            pltpu.VMEM(half, BF16),
            pltpu.VMEM(half, BF16),
            pltpu.VMEM((2,) + half, BF16),
            pltpu.VMEM((8, 2, QT, NH), BF16),
            pltpu.VMEM((4, 2, QT, NH), BF16),
            pltpu.VMEM((TB, GROUP), F32),
            pltpu.VMEM((2, 8 * QT, NH), BF16),
            pltpu.VMEM((8 * QT, GROUP), F32),
            pltpu.VMEM((8, QT, GROUP), F32),
            pltpu.VMEM((2, 3) + half, BF16),
            pltpu.VMEM((2, 3) + half, BF16),
            pltpu.VMEM((2,) + half, F32),
            pltpu.VMEM((2, 2, HB, NH), F32),
            pltpu.VMEM(half, BF16),
            pltpu.VMEM(half, BF16),
            pltpu.VMEM((2,) + half, BF16),
            pltpu.VMEM((GROUP, GROUP), BF16),
            pltpu.VMEM((2, NH, GROUP), BF16),
            pltpu.SemaphoreType.DMA((176,)),
            pltpu.SemaphoreType.DMA((176,)),
            pltpu.SemaphoreType.DMA((32,)),
        ],
        compiler_params=pltpu.CompilerParams(collective_id=0, has_side_effects=True, vmem_limit_bytes=56 * 2**20),
        cost_estimate=pl.CostEstimate(flops=7516192768, bytes_accessed=16 * 2**20, transcendentals=0),
    )(activations, quant_act, act_scale.T, act_mask, quant_weight, weight_mask, grad_out)
    return grad_act, grad_scale.T, grad_weight


def solution(mesh):
    return jax.shard_map(
        shards,
        mesh=mesh,
        in_specs=(
            P("dp", "tensor"),
            P("dp", "tensor"),
            P("dp", "tensor"),
            P("dp", "tensor"),
            P("dp", "tensor"),
            P("dp", "tensor"),
            P("dp", None),
        ),
        out_specs=(P("dp", "tensor"), P("dp", "tensor"), P("dp", "tensor")),
        check_vma=False,
    )
```

time: 106 us -> 91 us (0.86)
  Pallas kernels: 98.7 us -> 86 us
  local copies, waits for them, and re-layouts: 6.24 us -> 3.78 us
    pallas_call x1, Pallas kernels: 98.7 us -> 86 us  [shards(): pl.pallas_call(kernel, out_shape=(jax.ShapeDtypeStruct((TB, 2 * NH), BF16...]
    pallas_call x1 -> x0, local copies, waits for them, and re-layouts: 1.67 us -> none  [shards(): pl.pallas_call(kernel, out_shape=(jax.ShapeDtypeStruct((TB, 2 * NH), BF16...]
    unnamed x5 -> x7, local copies, waits for them, and re-layouts: 4.57 us -> 3.78 us
where the time goes in v2:
time: 91 us; the launch traced here: 90.4 us
  Pallas kernels  86 us (95%)
  local copies, waits for them, and re-layouts  3.78 us (4%)
    pallas_call x1, Pallas kernels, shards(): pl.pallas_call(kernel, out_shape=(jax.ShapeDtypeStruct((TB, 2 * NH), BF16...  86 us
    unnamed x7, local copies, waits for them, and re-layouts  3.78 us

profile of v2, /device:TPU:4, one launch (start us, length us, event | category | flops | bytes accessed | tf_op | source)
XLA Modules:
  0.0 90.4 jit_solution(3130431161230525326)
XLA Ops:
  0.6 86.0 %shard_map.94 = (bf16[256,1792]{1,0:T(8,128)(2,1)}, f32[14,256]{1,0:T(8,128)}, bf16[256,1792]{1,0:T(8,128)(2,1)}) custom-call(bf16[256,1792]{1,0:T(8,128)(2,1)} %act.1, bf16[256,1792]{1,0:T(8,128)(2,1)} %qa.1, f32[14,256]{1,0:T(8,128)} %bitcast.3, s32[256,1792]{1,0:T(8,128)} %mask.1, bf16[256,1792]{1,0:T(8,128)(2,1)} %w.1, s32[256,1792]{1,0:T(8,128)} %wmask.1, ...), custom_call_target="tpu_custom_call" | custom-call | flops 7516192768 | bytes 16777216 | tf_op jit(solution)/shard_map/pallas_call | solution.py:439
  86.6 0.0 copy-start.1
  86.6 0.0 copy-start
  86.6 2.2 %copy.13 = bf16[256,1792]{1,0:T(8,128)(2,1)} copy(bf16[256,1792]{1,0:T(8,128)(2,1)} %get-tuple-element.12) | data formatting | bytes 1835008
  88.9 0.0 copy-done.1
  88.9 0.6 copy.14
  89.5 0.0 copy-done
  89.5 0.9 %copy.15 = bf16[256,1792]{1,0:T(8,128)(2,1)} copy(bf16[256,1792]{1,0:T(8,128)(2,1)S(1)} %copy-done) | data formatting | bytes 1835008
Async XLA Ops:
  86.6 2.3 %copy-start.1 = (f32[14,256]{1,0:T(8,128)S(1)}, f32[14,256]{1,0:T(8,128)}, u32[]{:S(2)}) copy-start(f32[14,256]{1,0:T(8,128)} %get-tuple-element.7) | copy-start | bytes 43012
  86.6 2.9 %copy-start = (bf16[256,1792]{1,0:T(8,128)(2,1)S(1)}, bf16[256,1792]{1,0:T(8,128)(2,1)}, u32[]{:S(2)}) copy-start(bf16[256,1792]{1,0:T(8,128)(2,1)} %get-tuple-element.14) | copy-start | bytes 2752516

commit v3 on v2

--- a/solution.py
+++ b/solution.py
@@ -15,6 +15,7 @@
 QT = 64
 GH = NH // GROUP
 CHUNKS = ((0, 256), (256, 256), (512, 384))
+PARTS = 4
 MESH = pl.DeviceIdType.MESH
 F32 = jnp.float32
 BF16 = jnp.bfloat16
@@ -340,18 +341,17 @@
     quant_cross(1)
     w_complete(2)
     quant_start(0, 2)
+    quant_start(1, 2)
+    rotate(0, 2, quant_end(0, 2))
+    quant_cross(2)
     reduce_far(0)
-    rotate(0, 2, quant_end(0, 2))
-    quant_start(1, 2)
+    reduce_pass(1)
+    gq_x[0].wait_recv()
+    rotate(1, 0, gqx_recv[:, CHUNKS[0][0] : sum(CHUNKS[0])])
     reduce_near(0)
-    quant_cross(2)
-    gq_x[0].wait_recv()
-    rotate(1, 0, gqx_recv[:, 0:256])
-    reduce_pass(1)
+    dw_own[1] = weight_block(1, 0)
     gq_x[1].wait_recv()
-    rotate(1, 1, gqx_recv[:, 256:512])
-    reduce_pass(0)
-    dw_own[1] = weight_block(1, 0)
+    rotate(1, 1, gqx_recv[:, CHUNKS[1][0] : sum(CHUNKS[1])])
     dw_own[0] = weight_block(0, 0)
 
     sign = (1 - 2 * h).astype(F32)
@@ -390,12 +390,13 @@
             s_send[...] += sums
 
     mix(0, 0)
+    reduce_pass(0)
     gq_x[2].wait_recv()
-    rotate(1, 2, gqx_recv[:, 512:896])
+    rotate(1, 2, gqx_recv[:, CHUNKS[2][0] : sum(CHUNKS[2])])
     mix(0, 1)
-    mix(0, 2)
     dwx_send[...] = reduce_end(1).astype(BF16)
     dw_x = remote(dwx_send, dwx_recv, x_side)
+    mix(0, 2)
     mix(1, 0)
     mix(1, 1)
     mix(1, 2)
@@ -430,6 +431,22 @@
         copy.wait()
     for copy in started:
         copy.wait_send()
+
+
+def hand_over(act, weight, out_act, out_weight, held, sems):
+    parts = []
+    for k, (src, dst) in enumerate(((act, out_act), (weight, out_weight))):
+        for i in range(PARTS):
+            rows = pl.ds(i * (TB // PARTS), TB // PARTS)
+            come = pltpu.make_async_copy(src.at[rows], held.at[k, rows], sems.at[0, k, i])
+            leave = pltpu.make_async_copy(held.at[k, rows], dst.at[rows], sems.at[1, k, i])
+            come.start()
+            parts.append((come, leave))
+    for come, leave in parts:
+        come.wait()
+        leave.start()
+    for come, leave in parts:
+        leave.wait()
 
 
 def shards(activations, quant_act, act_scale, act_mask, quant_weight, weight_mask, grad_out):
@@ -482,6 +499,17 @@
         compiler_params=pltpu.CompilerParams(collective_id=0, has_side_effects=True, vmem_limit_bytes=56 * 2**20),
         cost_estimate=pl.CostEstimate(flops=7516192768, bytes_accessed=16 * 2**20, transcendentals=0),
     )(activations, quant_act, act_scale.T, act_mask, quant_weight, weight_mask, grad_out)
+    grad_act, grad_weight = pl.pallas_call(
+        hand_over,
+        out_shape=(jax.ShapeDtypeStruct((TB, 2 * NH), BF16),) * 2,
+        in_specs=[anywhere] * 2,
+        out_specs=(anywhere,) * 2,
+        scratch_shapes=[
+            pltpu.VMEM((2, TB, 2 * NH), BF16),
+            pltpu.SemaphoreType.DMA((2, 2, PARTS)),
+        ],
+        cost_estimate=pl.CostEstimate(flops=0, bytes_accessed=4 * TB * 2 * NH * 2, transcendentals=0),
+    )(grad_act, grad_weight)
     return grad_act, grad_scale.T, grad_weight
 
 

time: 91 us -> 89.4 us (0.982)
  local copies, waits for them, and re-layouts: 3.78 us -> 0.61 us
  Pallas kernels: 86 us -> 87 us
    unnamed x7 -> x3, local copies, waits for them, and re-layouts: 3.78 us -> 0.61 us
    pallas_call x0 -> x1, Pallas kernels: none -> 2.41 us  [shards(): pl.pallas_call(hand_over, out_shape=(jax.ShapeDtypeStruct((TB, 2 * NH), B...]
    pallas_call x1, Pallas kernels: 86 us -> 84.6 us  [shards(): pl.pallas_call(kernel, out_shape=(jax.ShapeDtypeStruct((TB, 2 * NH), BF16...]
where the time goes in v3:
time: 89.4 us; the launch traced here: 88.3 us
  Pallas kernels  87 us (97%)
    pallas_call x1, Pallas kernels, shards(): pl.pallas_call(kernel, out_shape=(jax.ShapeDtypeStruct((TB, 2 * NH), BF16...  84.6 us
    pallas_call x1, Pallas kernels, shards(): pl.pallas_call(hand_over, out_shape=(jax.ShapeDtypeStruct((TB, 2 * NH), B...  2.41 us

profile of v3, /device:TPU:4, one launch (start us, length us, event | category | flops | bytes accessed | tf_op | source)
XLA Modules:
  0.0 88.3 jit_solution(3674294506555181700)
XLA Ops:
  0.6 84.6 %shard_map.94 = (bf16[256,1792]{1,0:T(8,128)(2,1)}, f32[14,256]{1,0:T(8,128)}, bf16[256,1792]{1,0:T(8,128)(2,1)}) custom-call(bf16[256,1792]{1,0:T(8,128)(2,1)} %act.1, bf16[256,1792]{1,0:T(8,128)(2,1)} %qa.1, f32[14,256]{1,0:T(8,128)} %bitcast.3, s32[256,1792]{1,0:T(8,128)} %mask.1, bf16[256,1792]{1,0:T(8,128)(2,1)} %w.1, s32[256,1792]{1,0:T(8,128)} %wmask.1, ...), custom_call_target="tpu_custom_call" | custom-call | flops 7516192768 | bytes 16777216 | tf_op jit(solution)/shard_map/pallas_call | solution.py:456
  85.3 0.0 copy-start
  85.3 2.4 %shard_map.95 = (bf16[256,1792]{1,0:T(8,128)(2,1)}, bf16[256,1792]{1,0:T(8,128)(2,1)}) custom-call(bf16[256,1792]{1,0:T(8,128)(2,1)} %get-tuple-element.8.act, bf16[256,1792]{1,0:T(8,128)(2,1)} %get-tuple-element.9.weight), custom_call_target="tpu_custom_call" | custom-call | bytes 3670016 | tf_op jit(solution)/shard_map/pallas_call | solution.py:502
  87.7 0.0 copy-done
  87.7 0.6 copy.11
Async XLA Ops:
  85.3 2.4 %copy-start = (f32[14,256]{1,0:T(8,128)S(1)}, f32[14,256]{1,0:T(8,128)}, u32[]{:S(2)}) copy-start(f32[14,256]{1,0:T(8,128)} %get-tuple-element.11) | copy-start | bytes 43012

commit v4 on v3

--- a/solution.py
+++ b/solution.py
@@ -345,9 +345,9 @@
     rotate(0, 2, quant_end(0, 2))
     quant_cross(2)
     reduce_far(0)
-    reduce_pass(1)
     gq_x[0].wait_recv()
     rotate(1, 0, gqx_recv[:, CHUNKS[0][0] : sum(CHUNKS[0])])
+    reduce_pass(1)
     reduce_near(0)
     dw_own[1] = weight_block(1, 0)
     gq_x[1].wait_recv()

time: 89.4 us -> 89.4 us (level)
  no operation moved by 1% of the time
where the time goes in v4:
time: 89.4 us; the launch traced here: 88.3 us
  Pallas kernels  87 us (97%)
    pallas_call x1, Pallas kernels, shards(): pl.pallas_call(kernel, out_shape=(jax.ShapeDtypeStruct((TB, 2 * NH), BF16...  84.6 us
    pallas_call x1, Pallas kernels, shards(): pl.pallas_call(hand_over, out_shape=(jax.ShapeDtypeStruct((TB, 2 * NH), B...  2.41 us

profile of v4, /device:TPU:4, one launch (start us, length us, event | category | flops | bytes accessed | tf_op | source)
XLA Modules:
  0.0 88.3 jit_solution(14294956334630803086)
XLA Ops:
  0.6 84.6 %shard_map.94 = (bf16[256,1792]{1,0:T(8,128)(2,1)}, f32[14,256]{1,0:T(8,128)}, bf16[256,1792]{1,0:T(8,128)(2,1)}) custom-call(bf16[256,1792]{1,0:T(8,128)(2,1)} %act.1, bf16[256,1792]{1,0:T(8,128)(2,1)} %qa.1, f32[14,256]{1,0:T(8,128)} %bitcast.3, s32[256,1792]{1,0:T(8,128)} %mask.1, bf16[256,1792]{1,0:T(8,128)(2,1)} %w.1, s32[256,1792]{1,0:T(8,128)} %wmask.1, ...), custom_call_target="tpu_custom_call" | custom-call | flops 7516192768 | bytes 16777216 | tf_op jit(solution)/shard_map/pallas_call | solution.py:456
  85.3 0.0 copy-start
  85.3 2.4 %shard_map.95 = (bf16[256,1792]{1,0:T(8,128)(2,1)}, bf16[256,1792]{1,0:T(8,128)(2,1)}) custom-call(bf16[256,1792]{1,0:T(8,128)(2,1)} %get-tuple-element.8.act, bf16[256,1792]{1,0:T(8,128)(2,1)} %get-tuple-element.9.weight), custom_call_target="tpu_custom_call" | custom-call | bytes 3670016 | tf_op jit(solution)/shard_map/pallas_call | solution.py:502
  87.7 0.0 copy-done
  87.7 0.6 copy.11
Async XLA Ops:
  85.3 2.4 %copy-start = (f32[14,256]{1,0:T(8,128)S(1)}, f32[14,256]{1,0:T(8,128)}, u32[]{:S(2)}) copy-start(f32[14,256]{1,0:T(8,128)} %get-tuple-element.11) | copy-start | bytes 43012
